TPU v7x, 512 devices: a whole 4x8x8 slice. The times are simulated.
512 devices in a mesh: dp: 2 (over z_hi), ctx: 32 (over y, z_lo), tensor: 8 (over x, core).
Axes of the slice: x: 4, y: 8, z: 8 (z_hi: 2, z_lo: 4; z = z_hi * 4 + z_lo), core: 2. Of those that a mesh axis runs over, the one named last changes fastest.
Arguments:
- left_gate: bfloat16 [2, 4096, 4096], P('dp', 'ctx', 'tensor'), may hold values from -6 to 6
- right_gate: bfloat16 [2, 4096, 4096], P('dp', 'ctx', 'tensor'), may hold values from -6 to 6
- values: bfloat16 [2, 4096, 4096], P('dp', 'ctx', 'tensor'), may hold values from -6 to 6
- grad_out: bfloat16 [2, 4096, 4096], P('dp', 'ctx', 'tensor'), may hold values from -6 to 6
- residues: float32 [256, 16], replicated, may hold values from -0.09375 to 0.09375
- decay_rates: float32 [256, 16], replicated, may hold values from 0.5 to 128
Outputs:
- gated_out: bfloat16 [2, 4096, 4096], P('dp', 'ctx', 'tensor')
- grad_left: bfloat16 [2, 4096, 4096], P('dp', 'ctx', 'tensor')
- grad_right: bfloat16 [2, 4096, 4096], P('dp', 'ctx', 'tensor')
- grad_values: bfloat16 [2, 4096, 4096], P('dp', 'ctx', 'tensor')
- grad_residues: float32 [256, 16], replicated
- grad_rates: float32 [256, 16], replicated
All inputs are finite; a program needn't handle non-finite values.
Results may differ from a plain program's by a relative error of at most 0.0065.
Values may be sent and summed in bfloat16 or wider, within the bound.
A program may use at most 64 MiB of HBM per device.

v0:
```python
import functools

import jax
import jax.numpy as jnp
from jax import lax
from jax.experimental import pallas as pl
from jax.experimental.pallas import tpu as pltpu
from jax.sharding import PartitionSpec as P

MESH = pl.DeviceIdType.MESH
BF = jnp.bfloat16
F32 = jnp.float32
GSIZE = 16
ORD = 16
TILE = 128
PER_TILE = TILE // GSIZE
CLIP = 32.0
NT = (((1,), (1,)), ((), ()))
NN = (((1,), (0,)), ((), ()))


def dot(a, b, dims=NN):
    return lax.dot_general(a, b, dims, preferred_element_type=F32)


def split(x):
    hi = x.astype(BF)
    return hi, (x - hi.astype(F32)).astype(BF)


def lanes8(x):
    return jnp.concatenate([x] * PER_TILE, axis=1)


def shift(x, amount):
    amount = amount % TILE
    return x if amount == 0 else pltpu.roll(x, amount, 1)


def decays(rate, positions, top=None):
    sub = lax.broadcasted_iota(jnp.int32, (8, TILE), 0).astype(F32)
    blocks = positions // 8
    step = jnp.exp(-8.0 * rate)
    now = jnp.exp(-rate * (sub if top is None else top - (positions - 8) - sub))
    rows = [now]
    for _ in range(blocks - 1):
        now = now * step
        rows.append(now)
    if top is not None:
        rows = rows[::-1]
    return jnp.concatenate(rows, axis=0)


def kernel(
    n_ctx,
    n_tensor,
    n_dp,
    left_hbm,
    right_hbm,
    values_hbm,
    grad_hbm,
    res_hbm,
    rate_hbm,
    out_conv,
    out_left,
    out_right,
    out_values,
    out_res,
    out_rate,
    vin,
    par,
    gst,
    tables,
    taps,
    convs,
    msg1,
    recv1,
    lag1,
    lagr,
    msg2,
    recv2,
    msg3,
    recv3,
    vout,
    gout,
    in_sem,
    par_sem,
    send_sem,
    recv_sem,
    out_sem,
):
    me = lax.axis_index("ctx")
    my_t = lax.axis_index("tensor")
    my_d = lax.axis_index("dp")
    positions = vin.shape[2]
    tiles = vin.shape[1]
    seq = n_ctx * positions
    groups = tiles * PER_TILE
    n_side = n_dp * n_tensor
    my_side = my_d * n_tensor + my_t
    inv = 1.0 / seq

    barrier = pltpu.get_barrier_semaphore()

    def greet_ctx(o, carry):
        peer = lax.rem(me + o, n_ctx)
        pl.semaphore_signal(barrier, inc=1, device_id={"ctx": peer}, device_id_type=MESH)
        return carry

    lax.fori_loop(1, n_ctx, greet_ctx, 0)

    def greet_side(o, carry):
        peer = lax.rem(my_side + o, n_side)
        pl.semaphore_signal(
            barrier,
            inc=1,
            device_id={"dp": peer // n_tensor, "tensor": lax.rem(peer, n_tensor)},
            device_id_type=MESH,
        )
        return carry

    lax.fori_loop(1, n_side, greet_side, 0)

    for k, ref in enumerate((res_hbm, rate_hbm)):
        pltpu.make_async_copy(ref, gout.at[k], par_sem).start()
    for j in range(tiles):
        for a, ref in enumerate((left_hbm, values_hbm, right_hbm, grad_hbm)):
            pltpu.make_async_copy(
                ref.at[:, pl.ds(j * TILE, TILE)], vin.at[a, j], in_sem.at[j]
            ).start()
    pltpu.make_async_copy(gout, gout, par_sem).wait()
    for k in range(2):
        par[k] = gout[k].T
    first = pl.multiple_of(my_t * groups, groups)

    lane = lax.broadcasted_iota(jnp.int32, (8, TILE), 1)
    sub = lax.broadcasted_iota(jnp.int32, (8, TILE), 0)
    block = lane // GSIZE
    row_i = lax.broadcasted_iota(jnp.int32, (TILE, TILE), 0)
    col_i = lax.broadcasted_iota(jnp.int32, (TILE, TILE), 1)
    pos_col = row_i.astype(F32)

    pl.semaphore_wait(barrier, n_ctx - 1 + n_side - 1)

    def states(j, carry):
        pick = pl.ds(pl.multiple_of(first + j * PER_TILE, PER_TILE), PER_TILE)
        rates = jnp.where(block == sub, lanes8(par[1, pick, :]), 0.0)
        resid = jnp.where(block == sub, lanes8(par[0, pick, :]), 0.0)
        rate = jnp.sum(rates, axis=0, keepdims=True) * inv
        ahead = decays(rate, positions, positions)
        ahead1 = decays(shift(rate, 16), positions, positions) * (positions - pos_col)
        after2 = decays(shift(rate, 32), positions) * pos_col
        after = decays(shift(rate, 48), positions)
        q_hi, q_lo = split(ahead)
        p_hi, p_lo = split(after)
        tables[j, 0] = q_hi
        tables[j, 1] = q_lo
        tables[j, 2] = p_hi
        tables[j, 3] = p_lo
        r_hi, r_lo = split(shift(resid, 48))
        taps[j] = dot(r_hi, p_hi, NT) + (dot(r_lo, p_hi, NT) + dot(r_hi, p_lo, NT))

        pltpu.make_async_copy(vin.at[:, j], vin.at[:, j], in_sem.at[j]).wait()
        gated = (vin[0, j].astype(F32) * vin[1, j].astype(F32)).astype(BF)
        signal = (vin[2, j].astype(F32) * vin[3, j].astype(F32)).astype(BF)
        gst[0, j] = gated
        gst[1, j] = signal
        gated_t = gated.T
        signal_t = signal.T
        gst[2, j] = gated_t
        gst[3, j] = signal_t
        kinds = (
            dot(gated_t, q_hi) + dot(gated_t, q_lo),
            dot(gated_t, ahead1.astype(BF)),
            dot(signal_t, after2.astype(BF)),
            dot(signal_t, p_hi) + dot(signal_t, p_lo),
        )
        for g in range(PER_TILE):
            which = (block - g) & 7
            halves = []
            for half in range(2):
                at = g * GSIZE + 8 * half
                part = kinds[3][at : at + 8]
                for k in (2, 1, 0):
                    part = jnp.where(which == k, kinds[k][at : at + 8], part)
                halves.append(part)
            msg1[j * PER_TILE + g] = jnp.where(which < 4, halves[0], shift(halves[1], 64))
        return carry

    lax.fori_loop(0, tiles, states, 0)

    def exchange(src, dst, k):
        def one(o, carry):
            peer = lax.rem(me + o, n_ctx)
            pltpu.make_async_remote_copy(
                src_ref=src.at[peer],
                dst_ref=dst.at[me],
                send_sem=send_sem.at[k],
                recv_sem=recv_sem.at[k],
                device_id={"ctx": peer},
                device_id_type=MESH,
            ).start()
            return carry

        lax.fori_loop(1, n_ctx, one, 0)
        dst[me] = src[me]

    def landed(dst, k, count):
        part = dst.at[pl.ds(0, count)]
        pltpu.make_async_copy(part, part, recv_sem.at[k]).wait()

    def sent(src, k, count):
        part = src.at[pl.ds(0, count)]
        pltpu.make_async_copy(part, part, send_sem.at[k]).wait()

    exchange(msg1, recv1, 0)

    later = col_i >= row_i
    mirror = row_i + col_i
    flip = jnp.where(mirror == positions - 1, 1.0, 0.0).astype(BF)

    def lags(j, carry):
        gated = gst[0, j]
        signal = dot(flip, gst[1, j]).astype(BF)
        for g in range(PER_TILE):
            only = jnp.where(col_i // GSIZE == g, gated.astype(F32), 0.0).astype(BF)
            pair = jnp.where(mirror < positions, dot(only, signal, NT), 0.0)
            skew = pltpu.roll(pair, 0, 1, stride=1, stride_axis=0)
            lag1[j * PER_TILE + g] = jnp.sum(skew, axis=0, keepdims=True)
        return carry

    lax.fori_loop(0, tiles, lags, 0)
    exchange(lag1, lagr, 1)

    def inside(j, carry):
        rows = taps[j].astype(BF).astype(F32)
        for g in range(PER_TILE):
            wide = jnp.broadcast_to(rows[g : g + 1], (TILE, TILE))
            turned = pltpu.roll(wide, 0, 1, stride=1, stride_axis=0)
            upper = jnp.where(later, turned, 0.0).astype(BF)
            at = g * GSIZE
            convs[0, j, at : at + GSIZE, :] = dot(gst[2, j, at : at + GSIZE, :], upper)
            convs[1, j, at : at + GSIZE, :] = dot(gst[3, j, at : at + GSIZE, :], upper, NT)
        return carry

    lax.fori_loop(0, tiles, inside, 0)

    rate_d = lanes8(par[1, pl.ds(first + me, 1), :]) * inv
    res_d = lanes8(par[0, pl.ds(first + me, 1), :])
    decay_d = decays(rate_d, positions, positions - 1)
    dec = jnp.exp(-rate_d * positions)
    kind = (block - me) & 3
    is0, is1, is2, is3 = [kind == k for k in range(4)]

    landed(recv1, 0, n_ctx - 1)
    back = jnp.zeros((8, TILE), F32)
    for i in reversed(range(n_ctx)):
        msg2[i] = back
        back = back * dec + recv1[i]
    front = jnp.zeros((8, TILE), F32)
    sum_r = jnp.zeros((8, TILE), F32)
    sum_s = jnp.zeros((8, TILE), F32)
    sum_m = jnp.zeros((8, TILE), F32)
    for i in range(n_ctx):
        own = recv1[i]
        behind = msg2[i]
        behind0 = shift(behind, 80)
        own0 = shift(own, 80)
        mixed = shift(jnp.where(is2, own, behind), 96)
        sum_r = sum_r + front * own0
        sum_m = sum_m + front * behind0
        sum_s = sum_s + jnp.where(is0, front, own) * mixed
        msg2[i] = jnp.where(is0, behind0, shift(front, 48)) * res_d
        front = front * dec + own

    def fold(x):
        x = jnp.sum(x, axis=0, keepdims=True)
        return x + shift(x, 64)

    raw_r = fold(sum_r)
    raw_s = fold(jnp.where(is0, sum_s + (positions * dec) * sum_m, 0.0)) + shift(
        fold(jnp.where(is1, sum_s, 0.0)), 112
    )
    landed(lagr, 1, n_ctx - 1)
    lag = jnp.sum(lagr[...], axis=0)
    weighted = jnp.where(sub == 0, lag, jnp.where(sub == 1, lag * (positions - 1 - lane).astype(F32), 0.0))
    close = lax.dot_general(
        weighted, decay_d, NN, precision=lax.Precision.HIGHEST, preferred_element_type=F32
    )
    raw_r = shift(raw_r + close[0:1], 16)
    raw_s = shift((raw_s + close[1:2]) * res_d * (-inv), 32)
    grads = jnp.where(is1, raw_r, raw_s)
    keep = is0 | is3
    for i in range(n_ctx):
        msg2[i] = jnp.where(keep, msg2[i], grads)
    exchange(msg2, recv2, 2)
    landed(recv2, 2, n_ctx - 1)

    pack = jnp.zeros((8, TILE), F32)
    for g in range(groups):
        row, quarter = g % 8, g // 8
        moved = shift(recv2[g], 16 * (2 * quarter - row - 1))
        pack = jnp.where((sub == row) & (block // 2 == quarter), moved, pack)
    msg3[...] = pack

    def side(o, carry):
        peer = lax.rem(my_side + o, n_side)
        pltpu.make_async_remote_copy(
            src_ref=msg3,
            dst_ref=recv3.at[my_side],
            send_sem=send_sem.at[3],
            recv_sem=recv_sem.at[3],
            device_id={"dp": peer // n_tensor, "tensor": lax.rem(peer, n_tensor)},
            device_id_type=MESH,
        ).start()
        return carry

    lax.fori_loop(1, n_side, side, 0)
    recv3[my_side] = pack

    outs = (out_conv, out_left, out_right, out_values)

    def finish(j, carry):
        heads = []
        tails = []
        for g in range(PER_TILE):
            m = recv2[j * PER_TILE + g]
            turned = shift(m, 64)
            for part in (m, turned):
                tails.append(jnp.where(block == g, part, 0.0))
                heads.append(jnp.where(block == (g + 3) % 8, part, 0.0))
        h_hi, h_lo = split(jnp.concatenate(heads, axis=0))
        b_hi, b_lo = split(jnp.concatenate(tails, axis=0))
        q_hi, q_lo, p_hi, p_lo = [tables[j, k] for k in range(4)]
        conv = convs[0, j] + (
            dot(h_hi, p_hi, NT) + (dot(h_lo, p_hi, NT) + dot(h_hi, p_lo, NT))
        )
        conv_grad = convs[1, j] + (
            dot(b_hi, q_hi, NT) + (dot(b_lo, q_hi, NT) + dot(b_hi, q_lo, NT))
        )
        conv = conv.astype(BF).T.astype(F32)
        conv_grad = conv_grad.astype(BF).T.astype(F32)
        vout[0, j] = (vin[2, j].astype(F32) * conv).astype(BF)
        vout[1, j] = (conv_grad * vin[1, j].astype(F32)).astype(BF)
        vout[2, j] = (vin[3, j].astype(F32) * conv).astype(BF)
        vout[3, j] = (conv_grad * vin[0, j].astype(F32)).astype(BF)
        columns = pl.ds(pl.multiple_of(j * TILE, TILE), TILE)
        for a, ref in enumerate(outs):
            pltpu.make_async_copy(vout.at[a, j], ref.at[:, columns], out_sem.at[0]).start()
        return carry

    lax.fori_loop(0, tiles, finish, 0)

    landed(recv3, 3, n_side - 1)
    total = jnp.zeros((8, TILE), F32)
    summed = []
    for t in range(n_tensor):
        both = recv3[t]
        for d in range(1, n_dp):
            both = both + recv3[d * n_tensor + t]
        summed.append(both)
        total = total + both * both
    total = jnp.sum(jnp.sum(total, axis=0, keepdims=True), axis=1, keepdims=True)
    factor = CLIP / jnp.maximum(jnp.sqrt(total), CLIP)
    width = TILE // groups
    for at in range(0, n_tensor, width):
        rows = []
        for t in range(at, at + width):
            scaled = summed[t] * factor
            rows += [shift(scaled, -32 * quarter) for quarter in range(tiles)]
        turned = jnp.concatenate(rows, axis=0).T
        columns = slice(at * groups, (at + width) * groups)
        for k in range(2):
            gout[k, :, columns] = turned[k * ORD : (k + 1) * ORD]
    pltpu.make_async_copy(gout.at[0], out_res, out_sem.at[1]).start()
    pltpu.make_async_copy(gout.at[1], out_rate, out_sem.at[1]).start()

    sent(msg1, 0, n_ctx - 1)
    sent(lag1, 1, n_ctx - 1)
    sent(msg2, 2, n_ctx - 1)
    sent(recv3, 3, n_side - 1)
    pltpu.make_async_copy(vout, vout, out_sem.at[0]).wait()
    pltpu.make_async_copy(gout, gout, out_sem.at[1]).wait()


def solution(mesh):
    n_ctx, n_tensor, n_dp = mesh.shape["ctx"], mesh.shape["tensor"], mesh.shape["dp"]
    n_side = n_tensor * n_dp

    def on_device(left_gate, right_gate, values, grad_out, residues, decay_rates):
        positions, channels = left_gate.shape[1:]
        tiles = channels // TILE
        groups = channels // GSIZE
        flat = [x.reshape(positions, channels) for x in (left_gate, right_gate, values, grad_out)]
        wide = jax.ShapeDtypeStruct((positions, channels), BF)
        small = jax.ShapeDtypeStruct(residues.shape[::-1], F32)
        anywhere = pl.BlockSpec(memory_space=pl.ANY)
        outs = pl.pallas_call(
            functools.partial(kernel, n_ctx, n_tensor, n_dp),
            out_shape=(wide, wide, wide, wide, small, small),
            in_specs=[anywhere] * 6,
            out_specs=(anywhere,) * 6,
            scratch_shapes=[
                pltpu.VMEM((4, tiles, positions, TILE), BF),
                pltpu.VMEM((2,) + residues.shape, F32),
                pltpu.VMEM((4, tiles, TILE, TILE), BF),
                pltpu.VMEM((tiles, 4, positions, TILE), BF),
                pltpu.VMEM((tiles, PER_TILE, positions), F32),
                pltpu.VMEM((2, tiles, TILE, positions), F32),
                pltpu.VMEM((n_ctx, 8, TILE), F32),
                pltpu.VMEM((n_ctx, 8, TILE), F32),
                pltpu.VMEM((n_ctx, 1, TILE), F32),
                pltpu.VMEM((n_ctx, 1, TILE), F32),
                pltpu.VMEM((n_ctx, 8, TILE), F32),
                pltpu.VMEM((n_ctx, 8, TILE), F32),
                pltpu.VMEM((8, TILE), F32),
                pltpu.VMEM((n_side, 8, TILE), F32),
                pltpu.VMEM((4, tiles, positions, TILE), BF),
                pltpu.VMEM((2,) + residues.shape[::-1], F32),
                pltpu.SemaphoreType.DMA((tiles,)),
                pltpu.SemaphoreType.DMA,
                pltpu.SemaphoreType.DMA((4,)),
                pltpu.SemaphoreType.DMA((4,)),
                pltpu.SemaphoreType.DMA((2,)),
            ],
            compiler_params=pltpu.CompilerParams(
                collective_id=0, has_side_effects=True, vmem_limit_bytes=16 * 1024 * 1024
            ),
        )(*flat, residues.T, decay_rates.T)
        full = [x.reshape(1, positions, channels) for x in outs[:4]]
        return (*full, outs[4].T, outs[5].T)

    wide = P("dp", "ctx", "tensor")
    return jax.shard_map(
        on_device,
        mesh=mesh,
        in_specs=(wide, wide, wide, wide, P(), P()),
        out_specs=(wide, wide, wide, wide, P(), P()),
        check_vma=False,
    )
```

profile of v0, /device:TPU:1, one launch (start us, length us, event | category | flops | bytes accessed | tf_op | source)
XLA Modules:
  0.0 52.8 jit_solution(303906725234149992)
XLA Ops:
  0.6 0.0 copy-start
  0.6 0.9 %copy-done = bf16[1,128,512]{2,1,0:T(8,128)(2,1)S(1)} copy-done((bf16[1,128,512]{2,1,0:T(8,128)(2,1)S(1)}, bf16[1,128,512]{2,1,0:T(8,128)(2,1)}, u32[]{:S(2)}) %copy-start) | copy-done | bytes 131096
  1.5 0.0 copy-start.1
  1.5 0.9 %copy-done.1 = bf16[1,128,512]{2,1,0:T(8,128)(2,1)S(1)} copy-done((bf16[1,128,512]{2,1,0:T(8,128)(2,1)S(1)}, bf16[1,128,512]{2,1,0:T(8,128)(2,1)}, u32[]{:S(2)}) %copy-start.1) | copy-done | bytes 131096
  2.4 0.0 copy-start.2
  2.4 0.9 %copy-done.2 = bf16[1,128,512]{2,1,0:T(8,128)(2,1)S(1)} copy-done((bf16[1,128,512]{2,1,0:T(8,128)(2,1)S(1)}, bf16[1,128,512]{2,1,0:T(8,128)(2,1)}, u32[]{:S(2)}) %copy-start.2) | copy-done | bytes 131096
  3.3 0.0 copy-start.3
  3.4 0.9 %copy-done.3 = bf16[1,128,512]{2,1,0:T(8,128)(2,1)S(1)} copy-done((bf16[1,128,512]{2,1,0:T(8,128)(2,1)S(1)}, bf16[1,128,512]{2,1,0:T(8,128)(2,1)}, u32[]{:S(2)}) %copy-start.3) | copy-done | bytes 131096
  4.3 0.0 copy-start.4
  4.3 0.7 %copy-done.4 = f32[256,16]{0,1:T(8,128)S(1)} copy-done((f32[256,16]{0,1:T(8,128)S(1)}, f32[256,16]{0,1:T(8,128)}, u32[]{:S(2)}) %copy-start.4) | copy-done | bytes 16408
  5.0 0.0 copy-start.5
  5.0 0.7 %copy-done.5 = f32[256,16]{0,1:T(8,128)S(1)} copy-done((f32[256,16]{0,1:T(8,128)S(1)}, f32[256,16]{0,1:T(8,128)}, u32[]{:S(2)}) %copy-start.5) | copy-done | bytes 16408
  5.7 43.3 %shard_map.109 = (bf16[128,512]{1,0:T(8,128)(2,1)S(1)}, bf16[128,512]{1,0:T(8,128)(2,1)S(1)}, bf16[128,512]{1,0:T(8,128)(2,1)S(1)}, bf16[128,512]{1,0:T(8,128)(2...) custom-call(bf16[128,512]{1,0:T(8,128)(2,1)S(1)} %bitcast.12, bf16[128,512]{1,0:T(8,128)(2,1)S(1)} %bitcast.13, ...), custom_call_target="tpu_custom_call" | custom-call | tf_op jit(solution)/shard_map/pallas_call | solution.py:398
  49.0 0.7 %copy.18 = bf16[1,128,512]{2,1,0:T(8,128)(2,1)} copy(bf16[1,128,512]{2,1,0:T(8,128)(2,1)S(1)} %bitcast.19) | data formatting | bytes 262144
  49.7 0.7 %copy.19 = bf16[1,128,512]{2,1,0:T(8,128)(2,1)} copy(bf16[1,128,512]{2,1,0:T(8,128)(2,1)S(1)} %bitcast.18) | data formatting | bytes 262144
  50.3 0.7 %copy.20 = bf16[1,128,512]{2,1,0:T(8,128)(2,1)} copy(bf16[1,128,512]{2,1,0:T(8,128)(2,1)S(1)} %bitcast.17) | data formatting | bytes 262144
  51.0 0.7 %copy.21 = bf16[1,128,512]{2,1,0:T(8,128)(2,1)} copy(bf16[1,128,512]{2,1,0:T(8,128)(2,1)S(1)} %bitcast.16) | data formatting | bytes 262144
  51.6 0.6 %copy.22 = f32[256,16]{0,1:T(8,128)} copy(f32[256,16]{0,1:T(8,128)S(1)} %bitcast.23) | data formatting | bytes 32768
  52.2 0.6 %copy.23 = f32[256,16]{0,1:T(8,128)} copy(f32[256,16]{0,1:T(8,128)S(1)} %bitcast.22) | data formatting | bytes 32768
Async XLA Ops:
  0.6 0.9 %copy-start = (bf16[1,128,512]{2,1,0:T(8,128)(2,1)S(1)}, bf16[1,128,512]{2,1,0:T(8,128)(2,1)}, u32[]{:S(2)}) copy-start(bf16[1,128,512]{2,1,0:T(8,128)(2,1)} %param.6) | copy-start | bytes 393220
  1.5 0.9 %copy-start.1 = (bf16[1,128,512]{2,1,0:T(8,128)(2,1)S(1)}, bf16[1,128,512]{2,1,0:T(8,128)(2,1)}, u32[]{:S(2)}) copy-start(bf16[1,128,512]{2,1,0:T(8,128)(2,1)} %param.7) | copy-start | bytes 393220
  2.4 0.9 %copy-start.2 = (bf16[1,128,512]{2,1,0:T(8,128)(2,1)S(1)}, bf16[1,128,512]{2,1,0:T(8,128)(2,1)}, u32[]{:S(2)}) copy-start(bf16[1,128,512]{2,1,0:T(8,128)(2,1)} %param.8) | copy-start | bytes 393220
  3.3 0.9 %copy-start.3 = (bf16[1,128,512]{2,1,0:T(8,128)(2,1)S(1)}, bf16[1,128,512]{2,1,0:T(8,128)(2,1)}, u32[]{:S(2)}) copy-start(bf16[1,128,512]{2,1,0:T(8,128)(2,1)} %param.9) | copy-start | bytes 393220
  4.3 0.7 %copy-start.4 = (f32[256,16]{0,1:T(8,128)S(1)}, f32[256,16]{0,1:T(8,128)}, u32[]{:S(2)}) copy-start(f32[256,16]{0,1:T(8,128)} %param.10) | copy-start | bytes 49156
  5.0 0.7 %copy-start.5 = (f32[256,16]{0,1:T(8,128)S(1)}, f32[256,16]{0,1:T(8,128)}, u32[]{:S(2)}) copy-start(f32[256,16]{0,1:T(8,128)} %param.11) | copy-start | bytes 49156
where the time goes:
time: 53.1 us; the launch traced here: 52.8 us
  Pallas kernels  43.3 us (82%)
  local copies, waits for them, and re-layouts  8.87 us (17%)
  between operations  0.66 us (1%)
    pallas_call x1, Pallas kernels, on_device(): pl.pallas_call(functools.partial(kernel, n_ctx, n_tensor, n_dp), out_shap...  43.3 us
    unnamed x18, local copies, waits for them, and re-layouts  8.87 us

commit v1 on v0

v1 whole, which is shorter than its diff:
```python
import functools

import jax
import jax.numpy as jnp
from jax import lax
from jax.experimental import pallas as pl
from jax.experimental.pallas import tpu as pltpu
from jax.sharding import PartitionSpec as P

MESH = pl.DeviceIdType.MESH
BF = jnp.bfloat16
F32 = jnp.float32
GSIZE = 16
ORD = 16
TILE = 128
PER_TILE = TILE // GSIZE
CLIP = 32.0
N_Z = 4
N_CORE = 2
NT = (((1,), (1,)), ((), ()))
NN = (((1,), (0,)), ((), ()))


def dot(a, b, dims=NN):
    return lax.dot_general(a, b, dims, preferred_element_type=F32)


def split(x):
    hi = x.astype(BF)
    return hi, (x - hi.astype(F32)).astype(BF)


def lanes8(x):
    return jnp.concatenate([x] * PER_TILE, axis=1)


def shift(x, amount):
    amount = amount % TILE
    return x if amount == 0 else pltpu.roll(x, amount, 1)


def decays(rate, positions, top=None):
    sub = lax.broadcasted_iota(jnp.int32, (8, TILE), 0).astype(F32)
    blocks = positions // 8
    step = jnp.exp(-8.0 * rate)
    now = jnp.exp(-rate * (sub if top is None else top - (positions - 8) - sub))
    rows = [now]
    for _ in range(blocks - 1):
        now = now * step
        rows.append(now)
    if top is not None:
        rows = rows[::-1]
    return jnp.concatenate(rows, axis=0)


def kernel(
    n_ctx,
    n_z,
    n_tensor,
    n_core,
    n_dp,
    left_hbm,
    right_hbm,
    values_hbm,
    grad_hbm,
    res_hbm,
    rate_hbm,
    vout,
    gout,
    vin,
    par,
    gst,
    tables,
    taps,
    convs,
    msg1,
    recv1,
    msg2,
    recv2,
    grad1,
    gather1,
    grad2,
    gather2,
    in_sem,
    par_sem,
    send_sem,
    recv_sem,
):
    me = lax.axis_index("ctx")
    my_t = lax.axis_index("tensor")
    my_d = lax.axis_index("dp")
    positions = vin.shape[2]
    tiles = vin.shape[1]
    seq = n_ctx * positions
    groups = tiles * PER_TILE
    inv = 1.0 / seq

    for k, ref in enumerate((res_hbm, rate_hbm)):
        pltpu.make_async_copy(ref, gout.at[k], par_sem).start()
    for j in range(tiles):
        for a, ref in enumerate((left_hbm, values_hbm, right_hbm, grad_hbm)):
            pltpu.make_async_copy(
                ref.at[:, pl.ds(j * TILE, TILE)], vin.at[a, j], in_sem
            ).start()

    my_y, my_z = me // n_z, lax.rem(me, n_z)
    my_x, my_c = my_t // n_core, lax.rem(my_t, n_core)
    n_y, n_x = n_ctx // n_z, n_tensor // n_core
    ring = sorted(range(n_y), key=lambda o: -min(o, n_y - o))
    line = [
        (lax.rem(my_y + dy, n_y) * n_z + lax.rem(my_z + dz, n_z))
        for dy in ring
        for dz in reversed(range(n_z))
        if dy or dz
    ]
    first_set = [(peer, {"ctx": peer}) for peer in line]

    def spread(dd, dx, dz):
        d, x, z = lax.rem(my_d + dd, n_dp), lax.rem(my_x + dx, n_x), lax.rem(my_z + dz, n_z)
        where = {"dp": d, "tensor": x * n_core + my_c, "ctx": my_y * n_z + z}
        return (d * n_x + x) * n_z + z, where

    second_set = [
        spread(dd, dx, dz)
        for dd in reversed(range(n_dp))
        for dx in sorted(range(n_x), key=lambda o: -min(o, n_x - o))
        for dz in reversed(range(n_z))
        if dd or dx or dz
    ]
    new_second = [
        where
        for (_, where), (dd, dx) in zip(
            second_set,
            [
                (dd, dx)
                for dd in reversed(range(n_dp))
                for dx in sorted(range(n_x), key=lambda o: -min(o, n_x - o))
                for dz in reversed(range(n_z))
                if dd or dx or dz
            ],
        )
        if dd or dx
    ]

    def across(dy, dc):
        y, c = lax.rem(my_y + dy, n_y), lax.rem(my_c + dc, n_core)
        return c * n_y + y, {"tensor": my_x * n_core + c, "ctx": y * n_z + my_z}

    third_set = [across(dy, dc) for dy in ring for dc in reversed(range(n_core)) if dy or dc]
    new_third = [across(dy, dc)[1] for dy in ring for dc in range(1, n_core)]

    barrier = pltpu.get_barrier_semaphore()
    greeted = [where for _, where in first_set] + new_second + new_third
    for where in greeted:
        pl.semaphore_signal(barrier, inc=1, device_id=where, device_id_type=MESH)

    pltpu.make_async_copy(gout, gout, par_sem).wait()
    for k in range(2):
        par[k] = gout[k].T
    first = pl.multiple_of(my_t * groups, groups)

    lane = lax.broadcasted_iota(jnp.int32, (8, TILE), 1)
    sub = lax.broadcasted_iota(jnp.int32, (8, TILE), 0)
    block = lane // GSIZE
    row_i = lax.broadcasted_iota(jnp.int32, (TILE, TILE), 0)
    col_i = lax.broadcasted_iota(jnp.int32, (TILE, TILE), 1)
    pos_col = row_i.astype(F32)

    slopes = []
    for j in range(tiles):
        pick = pl.ds(pl.multiple_of(first + j * PER_TILE, PER_TILE), PER_TILE)
        rates = jnp.where(block == sub, lanes8(par[1, pick, :]), 0.0)
        resid = jnp.where(block == sub, lanes8(par[0, pick, :]), 0.0)
        rate = jnp.sum(rates, axis=0, keepdims=True) * inv
        ahead = decays(rate, positions, positions)
        ahead1 = decays(shift(rate, 16), positions, positions) * (positions - pos_col)
        after2 = decays(shift(rate, 32), positions) * pos_col
        after = decays(shift(rate, 48), positions)
        q_hi, q_lo = split(ahead)
        p_hi, p_lo = split(after)
        tables[j, 0] = q_hi
        tables[j, 1] = q_lo
        tables[j, 2] = p_hi
        tables[j, 3] = p_lo
        tables[j, 4] = ahead1.astype(BF)
        tables[j, 5] = after2.astype(BF)
        r_hi, r_lo = split(shift(resid, 48))
        taps[j] = dot(r_hi, p_hi, NT) + (dot(r_lo, p_hi, NT) + dot(r_hi, p_lo, NT))

    pltpu.make_async_copy(vin, vin, in_sem).wait()
    mirror = row_i + col_i
    flip = jnp.where(mirror == positions - 1, 1.0, 0.0).astype(BF)
    for j in range(tiles):
        gated = (vin[0, j].astype(F32) * vin[1, j].astype(F32)).astype(BF)
        signal = (vin[2, j].astype(F32) * vin[3, j].astype(F32)).astype(BF)
        gst[0, j] = gated
        gst[1, j] = dot(flip, signal).astype(BF)
        gated_t = gated.T
        signal_t = signal.T
        gst[2, j] = gated_t
        gst[3, j] = signal_t
        kinds = (
            dot(gated_t, tables[j, 0]) + dot(gated_t, tables[j, 1]),
            dot(gated_t, tables[j, 4]),
            dot(signal_t, tables[j, 5]),
            dot(signal_t, tables[j, 2]) + dot(signal_t, tables[j, 3]),
        )
        for g in range(PER_TILE):
            which = (block - g) & 7
            halves = []
            for half in range(2):
                at = g * GSIZE + 8 * half
                part = kinds[3][at : at + 8]
                for k in (2, 1, 0):
                    part = jnp.where(which == k, kinds[k][at : at + 8], part)
                halves.append(part)
            msg1[j * PER_TILE + g, 0:8, :] = jnp.where(
                which < 4, halves[0], shift(halves[1], 64)
            )

    for j in range(tiles):
        gated = gst[0, j]
        flipped = gst[1, j]
        for g in range(PER_TILE):
            only = jnp.where(col_i // GSIZE == g, gated.astype(F32), 0.0).astype(BF)
            pair = jnp.where(mirror < positions, dot(only, flipped, NT), 0.0)
            skew = pltpu.roll(pair, 0, 1, stride=1, stride_axis=0)
            msg1[j * PER_TILE + g, 8:9, :] = jnp.sum(skew, axis=0, keepdims=True)

    def send(src, dst, mine, peers, k):
        for slot, where in peers:
            pltpu.make_async_remote_copy(
                src_ref=src.at[slot] if len(src.shape) == len(dst.shape) else src,
                dst_ref=dst.at[mine],
                send_sem=send_sem.at[k],
                recv_sem=recv_sem.at[k],
                device_id=where,
                device_id_type=MESH,
            ).start()

    def landed(dst, k, peers):
        part = dst.at[pl.ds(0, len(peers))]
        pltpu.make_async_copy(part, part, recv_sem.at[k]).wait()

    def sent(dst, k, peers):
        part = dst.at[pl.ds(0, len(peers))]
        pltpu.make_async_copy(part, part, send_sem.at[k]).wait()

    pl.semaphore_wait(barrier, len(greeted))
    send(msg1, recv1, me, first_set, 0)
    recv1[me] = msg1[me]

    later = col_i >= row_i

    def inside(j, carry):
        rows = taps[j].astype(BF).astype(F32)
        for g in range(PER_TILE):
            wide = jnp.broadcast_to(rows[g : g + 1], (TILE, TILE))
            turned = pltpu.roll(wide, 0, 1, stride=1, stride_axis=0)
            upper = jnp.where(later, turned, 0.0).astype(BF)
            at = g * GSIZE
            convs[0, j, at : at + GSIZE, :] = dot(gst[2, j, at : at + GSIZE, :], upper)
            convs[1, j, at : at + GSIZE, :] = dot(gst[3, j, at : at + GSIZE, :], upper, NT)
        return carry

    lax.fori_loop(0, tiles, inside, 0)

    rate_d = lanes8(par[1, pl.ds(first + me, 1), :]) * inv
    res_d = lanes8(par[0, pl.ds(first + me, 1), :])
    decay_d = decays(rate_d, positions, positions - 1)
    dec = jnp.exp(-rate_d * positions)
    kind = (block - me) & 3
    is0, is1, is2, is3 = [kind == k for k in range(4)]

    landed(recv1, 0, first_set)
    back = jnp.zeros((8, TILE), F32)
    for i in reversed(range(n_ctx)):
        msg2[i] = back
        back = back * dec + recv1[i, 0:8, :]
    front = jnp.zeros((8, TILE), F32)
    sum_r = jnp.zeros((8, TILE), F32)
    sum_s = jnp.zeros((8, TILE), F32)
    sum_m = jnp.zeros((8, TILE), F32)
    for i in range(n_ctx):
        own = recv1[i, 0:8, :]
        behind = msg2[i]
        behind0 = shift(behind, 80)
        own0 = shift(own, 80)
        mixed = shift(jnp.where(is2, own, behind), 96)
        sum_r = sum_r + front * own0
        sum_m = sum_m + front * behind0
        sum_s = sum_s + jnp.where(is0, front, own) * mixed
        msg2[i] = jnp.where(is0, behind0, shift(front, 48)) * res_d
        front = front * dec + own
    send(msg2, recv2, me, first_set, 1)
    recv2[me] = msg2[me]

    def fold(x):
        x = jnp.sum(x, axis=0, keepdims=True)
        return x + shift(x, 64)

    raw_r = fold(sum_r)
    raw_s = fold(jnp.where(is0, sum_s + (positions * dec) * sum_m, 0.0)) + shift(
        fold(jnp.where(is1, sum_s, 0.0)), 112
    )
    lag = jnp.sum(recv1[:, 8:9, :], axis=0)
    weighted = jnp.where(
        sub == 0, lag, jnp.where(sub == 1, lag * (positions - 1 - lane).astype(F32), 0.0)
    )
    shared = lax.dot_general(
        weighted, decay_d, NN, precision=lax.Precision.HIGHEST, preferred_element_type=F32
    )
    raw_r = jnp.where(is0[0:1], raw_r, 0.0)
    raw_s = jnp.where(is0[0:1], raw_s, 0.0)
    raw_r = raw_r + shift(raw_r, 32)
    raw_s = raw_s + shift(raw_s, 32)
    raw_r = raw_r + shift(raw_r, 16) + shared[0:1]
    raw_s = (raw_s + shift(raw_s, 16) + shared[1:2]) * res_d * (-inv)
    grads = jnp.where(block[0:1] % 2 == 0, raw_r, raw_s)
    my_second = (my_d * n_x + my_x) * n_z + my_z
    my_third = my_c * n_y + my_y
    grad1[...] = grads
    send(grad1, gather1, my_second, second_set, 2)
    gather1[my_second] = grads
    landed(gather1, 2, second_set)
    quarter = lax.broadcasted_iota(jnp.int32, (n_z, TILE), 1) // 32
    pack = jnp.zeros((n_z, TILE), F32)
    for x in range(n_x):
        both = gather1[x * n_z : (x + 1) * n_z, 0, :]
        for d in range(1, n_dp):
            at = (d * n_x + x) * n_z
            both = both + gather1[at : at + n_z, 0, :]
        pack = jnp.where(quarter == x, both, pack)
    grad2[...] = pack
    send(grad2, gather2, my_third, third_set, 3)
    gather2[my_third] = pack
    landed(recv2, 1, first_set)

    def finish(j, carry):
        heads = []
        tails = []
        for g in range(PER_TILE):
            m = recv2[j * PER_TILE + g]
            turned = shift(m, 64)
            for part in (m, turned):
                tails.append(jnp.where(block == g, part, 0.0))
                heads.append(jnp.where(block == (g + 3) % 8, part, 0.0))
        h_hi, h_lo = split(jnp.concatenate(heads, axis=0))
        b_hi, b_lo = split(jnp.concatenate(tails, axis=0))
        q_hi, q_lo, p_hi, p_lo = [tables[j, k] for k in range(4)]
        conv = convs[0, j] + (
            dot(h_hi, p_hi, NT) + (dot(h_lo, p_hi, NT) + dot(h_hi, p_lo, NT))
        )
        conv_grad = convs[1, j] + (
            dot(b_hi, q_hi, NT) + (dot(b_lo, q_hi, NT) + dot(b_hi, q_lo, NT))
        )
        conv = conv.astype(BF).T.astype(F32)
        conv_grad = conv_grad.astype(BF).T.astype(F32)
        vout[0, j] = (vin[2, j].astype(F32) * conv).astype(BF)
        vout[1, j] = (conv_grad * vin[1, j].astype(F32)).astype(BF)
        vout[2, j] = (vin[3, j].astype(F32) * conv).astype(BF)
        vout[3, j] = (conv_grad * vin[0, j].astype(F32)).astype(BF)
        return carry

    lax.fori_loop(0, tiles, finish, 0)

    landed(gather2, 3, third_set)
    every = jnp.concatenate([gather2[i] for i in range(n_y * n_core)], axis=0)
    total = jnp.sum(jnp.sum(every * every, axis=0, keepdims=True), axis=1, keepdims=True)
    factor = CLIP / jnp.maximum(jnp.sqrt(total), CLIP)
    turned = (every * factor).T
    span = n_y * n_core * n_z
    for x in range(n_x):
        for k in range(2):
            at = x * 32 + k * ORD
            gout[k, :, x * span : (x + 1) * span] = turned[at : at + ORD]
    sent(recv1, 0, first_set)
    sent(recv2, 1, first_set)
    sent(gather1, 2, second_set)
    sent(gather2, 3, third_set)


def write_out(wide, small, out_conv, out_left, out_right, out_values, out_res, out_rate, sem):
    tiles = wide.shape[1]
    copies = [
        pltpu.make_async_copy(wide.at[a, j], ref.at[:, pl.ds(j * TILE, TILE)], sem)
        for a, ref in enumerate((out_conv, out_left, out_right, out_values))
        for j in range(tiles)
    ] + [pltpu.make_async_copy(small.at[k], ref, sem) for k, ref in enumerate((out_res, out_rate))]
    for copy in copies:
        copy.start()
    pltpu.make_async_copy(wide, wide, sem).wait()
    pltpu.make_async_copy(small, small, sem).wait()


def solution(mesh):
    n_ctx, n_tensor, n_dp = mesh.shape["ctx"], mesh.shape["tensor"], mesh.shape["dp"]

    def on_device(left_gate, right_gate, values, grad_out, residues, decay_rates):
        positions, channels = left_gate.shape[1:]
        tiles = channels // TILE
        groups = channels // GSIZE
        flat = [x.reshape(positions, channels) for x in (left_gate, right_gate, values, grad_out)]
        wide = jax.ShapeDtypeStruct((positions, channels), BF)
        small = jax.ShapeDtypeStruct(residues.shape[::-1], F32)
        in_hbm = pl.BlockSpec(memory_space=pltpu.HBM)
        in_vmem = pl.BlockSpec(memory_space=pltpu.VMEM)
        outs = pl.pallas_call(
            functools.partial(kernel, n_ctx, N_Z, n_tensor, N_CORE, n_dp),
            out_shape=(
                jax.ShapeDtypeStruct((4, tiles, positions, TILE), BF),
                jax.ShapeDtypeStruct((2,) + residues.shape[::-1], F32),
            ),
            in_specs=[in_hbm] * 6,
            out_specs=(in_vmem, in_vmem),
            scratch_shapes=[
                pltpu.VMEM((4, tiles, positions, TILE), BF),
                pltpu.VMEM((2,) + residues.shape, F32),
                pltpu.VMEM((4, tiles, TILE, TILE), BF),
                pltpu.VMEM((tiles, 6, positions, TILE), BF),
                pltpu.VMEM((tiles, PER_TILE, positions), F32),
                pltpu.VMEM((2, tiles, TILE, positions), F32),
                pltpu.VMEM((n_ctx, 9, TILE), F32),
                pltpu.VMEM((n_ctx, 9, TILE), F32),
                pltpu.VMEM((n_ctx, 8, TILE), F32),
                pltpu.VMEM((n_ctx, 8, TILE), F32),
                pltpu.VMEM((1, TILE), F32),
                pltpu.VMEM((n_dp * n_tensor // N_CORE * N_Z, 1, TILE), F32),
                pltpu.VMEM((N_Z, TILE), F32),
                pltpu.VMEM((n_ctx // N_Z * N_CORE, N_Z, TILE), F32),
                pltpu.SemaphoreType.DMA,
                pltpu.SemaphoreType.DMA,
                pltpu.SemaphoreType.DMA((4,)),
                pltpu.SemaphoreType.DMA((4,)),
            ],
            compiler_params=pltpu.CompilerParams(
                collective_id=0, has_side_effects=True, vmem_limit_bytes=16 * 1024 * 1024
            ),
        )(*[pltpu.with_memory_space_constraint(x, pltpu.HBM) for x in (*flat, residues.T, decay_rates.T)])
        outs = pl.pallas_call(
            write_out,
            out_shape=(wide, wide, wide, wide, small, small),
            in_specs=[pl.BlockSpec(memory_space=pl.ANY)] * 2,
            out_specs=(in_hbm,) * 6,
            scratch_shapes=[pltpu.SemaphoreType.DMA],
            compiler_params=pltpu.CompilerParams(vmem_limit_bytes=1024 * 1024),
        )(*outs)
        full = [x.reshape(1, positions, channels) for x in outs[:4]]
        return (*full, outs[4].T, outs[5].T)

    wide = P("dp", "ctx", "tensor")
    return jax.shard_map(
        on_device,
        mesh=mesh,
        in_specs=(wide, wide, wide, wide, P(), P()),
        out_specs=(wide, wide, wide, wide, P(), P()),
        check_vma=False,
    )
```

time: 53.1 us -> 36.1 us (0.68)
  local copies, waits for them, and re-layouts: 8.87 us -> 0 us
  Pallas kernels: 43.3 us -> 35.2 us
    unnamed x18 -> x0, local copies, waits for them, and re-layouts: 8.87 us -> none
    pallas_call x1 -> x2, Pallas kernels: 43.3 us -> 35.2 us  [the longest x1 34.4 us: on_device(): pl.pallas_call(functools.partial(kernel, n_ctx, N_Z, n_tensor, N_CORE, n_...]
where the time goes in v1:
time: 36.1 us; the launch traced here: 35.9 us
  Pallas kernels  35.2 us (98%)
  between operations  0.64 us (2%)
    pallas_call x1, Pallas kernels, on_device(): pl.pallas_call(functools.partial(kernel, n_ctx, N_Z, n_tensor, N_CORE, n_...  34.4 us
    pallas_call x1, Pallas kernels, on_device(): pl.pallas_call(write_out, out_shape=(wide, wide, wide, wide, small, small...  0.79 us

profile of v1, /device:TPU:1, one launch (start us, length us, event | category | flops | bytes accessed | tf_op | source)
XLA Modules:
  0.0 35.9 jit_solution(13411207500720654488)
XLA Ops:
  0.6 34.4 %shard_map.109 = (bf16[4,4,128,128]{3,2,1,0:T(8,128)(2,1)S(1)}, f32[2,16,256]{2,1,0:T(8,128)S(1)}) custom-call(bf16[128,512]{1,0:T(8,128)(2,1)} %bitcast.12, bf16[128,512]{1,0:T(8,128)(2,1)} %bitcast.13, bf16[128,512]{1,0:T(8,128)(2,1)} %bitcast.14, bf16[128,512]{1,0:T(8,128)(2,1)} %bitcast.15, f32[16,256]{1,0:T(8,128)} %bitcast.16, f32[16,256]{1,0:T(8,128)} %bitcast.17), custom_call_target="tpu_custom_call" | custom-call | tf_op jit(solution)/shard_map/pallas_call | solution.py:408
  35.1 0.8 %shard_map.110 = (bf16[128,512]{1,0:T(8,128)(2,1)}, bf16[128,512]{1,0:T(8,128)(2,1)}, bf16[128,512]{1,0:T(8,128)(2,1)}, bf16[128,512]{1,0:T(8,128)(2,1)}, f32[16,256]{1,0:T(8,128)}, /*index=5*/f32[16,256]{1,0:T(8,128)}) custom-call(bf16[4,4,128,128]{3,2,1,0:T(8,128)(2,1)S(1)} %get-tuple-element.14.wide, f32[2,16,256]{2,1,0:T(8,128)S(1)} %get-tuple-element.15.small), custom_call_target="tpu_custom_call" | custom-call | tf_op jit(solution)/shard_map/pallas_call | solution.py:440

commit v2 on v1

--- a/solution.py
+++ b/solution.py
@@ -75,6 +75,7 @@
     convs,
     msg1,
     recv1,
+    hold,
     msg2,
     recv2,
     grad1,
@@ -89,19 +90,11 @@
     me = lax.axis_index("ctx")
     my_t = lax.axis_index("tensor")
     my_d = lax.axis_index("dp")
-    positions = vin.shape[2]
-    tiles = vin.shape[1]
+    positions = vin.shape[1]
+    tiles = vin.shape[2] // TILE
     seq = n_ctx * positions
     groups = tiles * PER_TILE
     inv = 1.0 / seq
-
-    for k, ref in enumerate((res_hbm, rate_hbm)):
-        pltpu.make_async_copy(ref, gout.at[k], par_sem).start()
-    for j in range(tiles):
-        for a, ref in enumerate((left_hbm, values_hbm, right_hbm, grad_hbm)):
-            pltpu.make_async_copy(
-                ref.at[:, pl.ds(j * TILE, TILE)], vin.at[a, j], in_sem
-            ).start()
 
     my_y, my_z = me // n_z, lax.rem(me, n_z)
     my_x, my_c = my_t // n_core, lax.rem(my_t, n_core)
@@ -113,47 +106,86 @@
         for dz in reversed(range(n_z))
         if dy or dz
     ]
-    first_set = [(peer, {"ctx": peer}) for peer in line]
-
-    def spread(dd, dx, dz):
-        d, x, z = lax.rem(my_d + dd, n_dp), lax.rem(my_x + dx, n_x), lax.rem(my_z + dz, n_z)
-        where = {"dp": d, "tensor": x * n_core + my_c, "ctx": my_y * n_z + z}
-        return (d * n_x + x) * n_z + z, where
-
-    second_set = [
-        spread(dd, dx, dz)
+    mids = tuple(range(1, n_z - 1))
+    n_mid = len(mids)
+    own = (my_z >= mids[0]) & (my_z <= mids[-1])
+    held = groups // (n_y * n_mid)
+    my_owner = my_y * n_mid + my_z - mids[0]
+
+    def owner(dy, m):
+        y = lax.rem(my_y + dy, n_y)
+        return y * n_mid + m - mids[0], y * n_z + m
+
+    owners = [owner(dy, m) for dy in ring if dy for m in mids]
+    near = [owner(0, m) for m in mids]
+
+    def spread(dd, dx, z):
+        d, x = lax.rem(my_d + dd, n_dp), lax.rem(my_x + dx, n_x)
+        return {"dp": d, "tensor": x * n_core + my_c, "ctx": my_y * n_z + z}
+
+    turns = [
+        (dd, dx)
         for dd in reversed(range(n_dp))
         for dx in sorted(range(n_x), key=lambda o: -min(o, n_x - o))
+    ]
+    second_set = [
+        spread(dd, dx, lax.rem(my_z + dz, n_z))
+        for dd, dx in turns
         for dz in reversed(range(n_z))
         if dd or dx or dz
     ]
-    new_second = [
-        where
-        for (_, where), (dd, dx) in zip(
-            second_set,
-            [
-                (dd, dx)
-                for dd in reversed(range(n_dp))
-                for dx in sorted(range(n_x), key=lambda o: -min(o, n_x - o))
-                for dz in reversed(range(n_z))
-                if dd or dx or dz
-            ],
-        )
-        if dd or dx
-    ]
 
     def across(dy, dc):
         y, c = lax.rem(my_y + dy, n_y), lax.rem(my_c + dc, n_core)
         return c * n_y + y, {"tensor": my_x * n_core + c, "ctx": y * n_z + my_z}
 
-    third_set = [across(dy, dc) for dy in ring for dc in reversed(range(n_core)) if dy or dc]
-    new_third = [across(dy, dc)[1] for dy in ring for dc in range(1, n_core)]
+    third_set = [across(dy, dc)[1] for dy in ring for dc in reversed(range(n_core)) if dy or dc]
 
     barrier = pltpu.get_barrier_semaphore()
-    greeted = [where for _, where in first_set] + new_second + new_third
-    for where in greeted:
+
+    def greet(where):
         pl.semaphore_signal(barrier, inc=1, device_id=where, device_id_type=MESH)
 
+    ends = (0, n_z - 1)
+
+    @pl.when(own)
+    def _():
+        for dy in ring:
+            for z in ends:
+                greet({"ctx": lax.rem(my_y + dy, n_y) * n_z + z})
+        for dd, dx in turns:
+            if dd or dx:
+                for z in ends:
+                    greet(spread(dd, dx, z))
+        greet({"ctx": my_y * n_z + mids[0] + mids[-1] - my_z})
+
+    for _, peer in owners:
+        greet({"ctx": peer})
+    for dd, dx in turns:
+        if dd or dx:
+            for z in mids:
+                greet(spread(dd, dx, z))
+    for dy in ring:
+        for dc in range(1, n_core):
+            greet(across(dy, dc)[1])
+
+    @pl.when(jnp.logical_not(own))
+    def _():
+        for dy in ring:
+            if dy:
+                greet(across(dy, 0)[1])
+        for _, peer in near:
+            greet({"ctx": peer})
+
+    n_side = n_dp * n_x
+    met_own = n_ctx - 1 + (n_side - 1) * n_z + n_y * (n_core - 1)
+    met_end = n_y * n_mid + (n_side - 1) * n_mid + n_y * n_core - 1
+    met = jnp.where(own, met_own, met_end)
+
+    for k, ref in enumerate((res_hbm, rate_hbm)):
+        pltpu.make_async_copy(ref, gout.at[k], par_sem).start()
+    for a, ref in enumerate((left_hbm, values_hbm, right_hbm, grad_hbm)):
+        pltpu.make_async_copy(ref, vin.at[a], in_sem).start()
     pltpu.make_async_copy(gout, gout, par_sem).wait()
     for k in range(2):
         par[k] = gout[k].T
@@ -191,8 +223,8 @@
     mirror = row_i + col_i
     flip = jnp.where(mirror == positions - 1, 1.0, 0.0).astype(BF)
     for j in range(tiles):
-        gated = (vin[0, j].astype(F32) * vin[1, j].astype(F32)).astype(BF)
-        signal = (vin[2, j].astype(F32) * vin[3, j].astype(F32)).astype(BF)
+        gated = (vin[0, :, j * TILE : (j + 1) * TILE].astype(F32) * vin[1, :, j * TILE : (j + 1) * TILE].astype(F32)).astype(BF)
+        signal = (vin[2, :, j * TILE : (j + 1) * TILE].astype(F32) * vin[3, :, j * TILE : (j + 1) * TILE].astype(F32)).astype(BF)
         gst[0, j] = gated
         gst[1, j] = dot(flip, signal).astype(BF)
         gated_t = gated.T
@@ -227,28 +259,39 @@
             skew = pltpu.roll(pair, 0, 1, stride=1, stride_axis=0)
             msg1[j * PER_TILE + g, 8:9, :] = jnp.sum(skew, axis=0, keepdims=True)
 
-    def send(src, dst, mine, peers, k):
-        for slot, where in peers:
-            pltpu.make_async_remote_copy(
-                src_ref=src.at[slot] if len(src.shape) == len(dst.shape) else src,
-                dst_ref=dst.at[mine],
-                send_sem=send_sem.at[k],
-                recv_sem=recv_sem.at[k],
-                device_id=where,
-                device_id_type=MESH,
-            ).start()
-
-    def landed(dst, k, peers):
-        part = dst.at[pl.ds(0, len(peers))]
-        pltpu.make_async_copy(part, part, recv_sem.at[k]).wait()
-
-    def sent(dst, k, peers):
-        part = dst.at[pl.ds(0, len(peers))]
-        pltpu.make_async_copy(part, part, send_sem.at[k]).wait()
-
-    pl.semaphore_wait(barrier, len(greeted))
-    send(msg1, recv1, me, first_set, 0)
-    recv1[me] = msg1[me]
+    def send(src, dst, where, k):
+        pltpu.make_async_remote_copy(
+            src_ref=src,
+            dst_ref=dst,
+            send_sem=send_sem.at[k],
+            recv_sem=recv_sem.at[k],
+            device_id=where,
+            device_id_type=MESH,
+        ).start()
+
+    def settle(sem, dst, count):
+        part = dst.at[pl.ds(0, count)]
+        pltpu.make_async_copy(part, part, sem).wait()
+
+    def by_role(sem, dst, count_own, count_end):
+        @pl.when(own)
+        def _():
+            settle(sem, dst, count_own)
+
+        @pl.when(jnp.logical_not(own))
+        def _():
+            settle(sem, dst, count_end)
+
+    n_owner = n_y * n_mid
+
+    pl.semaphore_wait(barrier, met)
+    for o, peer in owners:
+        send(msg1.at[pl.ds(held * o, held)], recv1.at[me], {"ctx": peer}, 0)
+    for o, peer in near:
+
+        @pl.when(peer != me)
+        def _():
+            send(msg1.at[pl.ds(held * o, held)], recv1.at[me], {"ctx": peer}, 0)
 
     later = col_i >= row_i
 
@@ -265,64 +308,83 @@
 
     lax.fori_loop(0, tiles, inside, 0)
 
-    rate_d = lanes8(par[1, pl.ds(first + me, 1), :]) * inv
-    res_d = lanes8(par[0, pl.ds(first + me, 1), :])
-    decay_d = decays(rate_d, positions, positions - 1)
-    dec = jnp.exp(-rate_d * positions)
-    kind = (block - me) & 3
-    is0, is1, is2, is3 = [kind == k for k in range(4)]
-
-    landed(recv1, 0, first_set)
-    back = jnp.zeros((8, TILE), F32)
-    for i in reversed(range(n_ctx)):
-        msg2[i] = back
-        back = back * dec + recv1[i, 0:8, :]
-    front = jnp.zeros((8, TILE), F32)
-    sum_r = jnp.zeros((8, TILE), F32)
-    sum_s = jnp.zeros((8, TILE), F32)
-    sum_m = jnp.zeros((8, TILE), F32)
-    for i in range(n_ctx):
-        own = recv1[i, 0:8, :]
-        behind = msg2[i]
-        behind0 = shift(behind, 80)
-        own0 = shift(own, 80)
-        mixed = shift(jnp.where(is2, own, behind), 96)
-        sum_r = sum_r + front * own0
-        sum_m = sum_m + front * behind0
-        sum_s = sum_s + jnp.where(is0, front, own) * mixed
-        msg2[i] = jnp.where(is0, behind0, shift(front, 48)) * res_d
-        front = front * dec + own
-    send(msg2, recv2, me, first_set, 1)
-    recv2[me] = msg2[me]
-
-    def fold(x):
-        x = jnp.sum(x, axis=0, keepdims=True)
-        return x + shift(x, 64)
-
-    raw_r = fold(sum_r)
-    raw_s = fold(jnp.where(is0, sum_s + (positions * dec) * sum_m, 0.0)) + shift(
-        fold(jnp.where(is1, sum_s, 0.0)), 112
-    )
-    lag = jnp.sum(recv1[:, 8:9, :], axis=0)
-    weighted = jnp.where(
-        sub == 0, lag, jnp.where(sub == 1, lag * (positions - 1 - lane).astype(F32), 0.0)
-    )
-    shared = lax.dot_general(
-        weighted, decay_d, NN, precision=lax.Precision.HIGHEST, preferred_element_type=F32
-    )
-    raw_r = jnp.where(is0[0:1], raw_r, 0.0)
-    raw_s = jnp.where(is0[0:1], raw_s, 0.0)
-    raw_r = raw_r + shift(raw_r, 32)
-    raw_s = raw_s + shift(raw_s, 32)
-    raw_r = raw_r + shift(raw_r, 16) + shared[0:1]
-    raw_s = (raw_s + shift(raw_s, 16) + shared[1:2]) * res_d * (-inv)
-    grads = jnp.where(block[0:1] % 2 == 0, raw_r, raw_s)
-    my_second = (my_d * n_x + my_x) * n_z + my_z
-    my_third = my_c * n_y + my_y
-    grad1[...] = grads
-    send(grad1, gather1, my_second, second_set, 2)
-    gather1[my_second] = grads
-    landed(gather1, 2, second_set)
+    @pl.when(own)
+    def _():
+        recv1[me] = msg1[pl.ds(held * my_owner, held)]
+        local = []
+        for k in range(held):
+            at = held * my_owner + k
+            rate_d = lanes8(par[1, pl.ds(first + at, 1), :]) * inv
+            res_d = lanes8(par[0, pl.ds(first + at, 1), :])
+            decay_d = decays(rate_d, positions, positions - 1)
+            local.append((rate_d, res_d, decay_d, (block - at) & 3))
+        settle(recv_sem.at[0], recv1, n_ctx - 1)
+        for k in range(held):
+            rate_d, res_d, decay_d, kind = local[k]
+            dec = jnp.exp(-rate_d * positions)
+            is0, is1, is2, is3 = [kind == v for v in range(4)]
+            outer = is0 | is3
+            back = jnp.zeros((8, TILE), F32)
+            for i in reversed(range(n_ctx)):
+                hold[k, i] = back
+                back = back * dec + recv1[i, k, 0:8, :]
+            front = jnp.zeros((8, TILE), F32)
+            sum_r = jnp.zeros((8, TILE), F32)
+            sum_s = jnp.zeros((8, TILE), F32)
+            sum_m = jnp.zeros((8, TILE), F32)
+            for i in range(n_ctx):
+                mine = recv1[i, k, 0:8, :]
+                behind = hold[k, i]
+                behind0 = shift(behind, 80)
+                mixed = shift(jnp.where(is2, mine, behind), 96)
+                sum_r = sum_r + front * shift(mine, 80)
+                sum_m = sum_m + front * behind0
+                sum_s = sum_s + jnp.where(is0, front, mine) * mixed
+                both = jnp.where(is0, behind0, shift(front, 48)) * res_d
+                low = shift(pltpu.roll(both, 4, 0), 32)
+                msg2[i, k] = jnp.where(outer, both, low)[0:4]
+                front = front * dec + mine
+
+            def fold(x):
+                x = jnp.sum(x, axis=0, keepdims=True)
+                return x + shift(x, 64)
+
+            raw_r = fold(sum_r)
+            raw_s = fold(jnp.where(is0, sum_s + (positions * dec) * sum_m, 0.0)) + shift(
+                fold(jnp.where(is1, sum_s, 0.0)), 112
+            )
+            lag = jnp.sum(recv1[:, k, 8:9, :], axis=0)
+            weighted = jnp.where(
+                sub == 0, lag, jnp.where(sub == 1, lag * (positions - 1 - lane).astype(F32), 0.0)
+            )
+            shared = lax.dot_general(
+                weighted, decay_d, NN, precision=lax.Precision.HIGHEST, preferred_element_type=F32
+            )
+            raw_r = jnp.where(is0[0:1], raw_r, 0.0)
+            raw_s = jnp.where(is0[0:1], raw_s, 0.0)
+            raw_r = raw_r + shift(raw_r, 32)
+            raw_s = raw_s + shift(raw_s, 32)
+            raw_r = raw_r + shift(raw_r, 16) + shared[0:1]
+            raw_s = (raw_s + shift(raw_s, 16) + shared[1:2]) * res_d * (-inv)
+            grad1[k] = jnp.where(block[0:1] % 2 == 0, raw_r, raw_s)
+        slot = ((my_d * n_x + my_x) * n_mid + my_z - mids[0]) * held
+        for where in second_set:
+            send(grad1, gather1.at[pl.ds(slot, held)], where, 2)
+        gather1[pl.ds(slot, held)] = grad1[...]
+        for peer in line:
+            send(msg2.at[peer], recv2.at[my_owner], {"ctx": peer}, 1)
+        recv2[my_owner] = msg2[me]
+
+    n_second = n_side * n_mid
+
+    @pl.when(own)
+    def _():
+        settle(recv_sem.at[2], gather1, (n_second - 1) * held)
+
+    @pl.when(jnp.logical_not(own))
+    def _():
+        settle(recv_sem.at[2], gather1, n_second * held)
+
     quarter = lax.broadcasted_iota(jnp.int32, (n_z, TILE), 1) // 32
     pack = jnp.zeros((n_z, TILE), F32)
     for x in range(n_x):
@@ -332,15 +394,19 @@
             both = both + gather1[at : at + n_z, 0, :]
         pack = jnp.where(quarter == x, both, pack)
     grad2[...] = pack
-    send(grad2, gather2, my_third, third_set, 3)
+    my_third = my_c * n_y + my_y
+    for where in third_set:
+        send(grad2, gather2.at[my_third], where, 3)
     gather2[my_third] = pack
-    landed(recv2, 1, first_set)
+    by_role(recv_sem.at[1], recv2, n_owner - 1, n_owner)
 
     def finish(j, carry):
         heads = []
         tails = []
         for g in range(PER_TILE):
-            m = recv2[j * PER_TILE + g]
+            at = j * PER_TILE + g
+            top = recv2[at // held, at % held]
+            m = jnp.concatenate([top, shift(top, 96)], axis=0)
             turned = shift(m, 64)
             for part in (m, turned):
                 tails.append(jnp.where(block == g, part, 0.0))
@@ -356,15 +422,16 @@
         )
         conv = conv.astype(BF).T.astype(F32)
         conv_grad = conv_grad.astype(BF).T.astype(F32)
-        vout[0, j] = (vin[2, j].astype(F32) * conv).astype(BF)
-        vout[1, j] = (conv_grad * vin[1, j].astype(F32)).astype(BF)
-        vout[2, j] = (vin[3, j].astype(F32) * conv).astype(BF)
-        vout[3, j] = (conv_grad * vin[0, j].astype(F32)).astype(BF)
+        vout[0, :, j * TILE : (j + 1) * TILE] = (vin[2, :, j * TILE : (j + 1) * TILE].astype(F32) * conv).astype(BF)
+        vout[1, :, j * TILE : (j + 1) * TILE] = (conv_grad * vin[1, :, j * TILE : (j + 1) * TILE].astype(F32)).astype(BF)
+        vout[2, :, j * TILE : (j + 1) * TILE] = (vin[3, :, j * TILE : (j + 1) * TILE].astype(F32) * conv).astype(BF)
+        vout[3, :, j * TILE : (j + 1) * TILE] = (conv_grad * vin[0, :, j * TILE : (j + 1) * TILE].astype(F32)).astype(BF)
         return carry
 
-    lax.fori_loop(0, tiles, finish, 0)
-
-    landed(gather2, 3, third_set)
+    for j in range(tiles):
+        finish(j, 0)
+
+    settle(recv_sem.at[3], gather2, len(third_set))
     every = jnp.concatenate([gather2[i] for i in range(n_y * n_core)], axis=0)
     total = jnp.sum(jnp.sum(every * every, axis=0, keepdims=True), axis=1, keepdims=True)
     factor = CLIP / jnp.maximum(jnp.sqrt(total), CLIP)
@@ -374,19 +441,28 @@
         for k in range(2):
             at = x * 32 + k * ORD
             gout[k, :, x * span : (x + 1) * span] = turned[at : at + ORD]
-    sent(recv1, 0, first_set)
-    sent(recv2, 1, first_set)
-    sent(gather1, 2, second_set)
-    sent(gather2, 3, third_set)
+    by_role(send_sem.at[0], recv1, n_owner - 1, n_owner)
+
+    @pl.when(own)
+    def _():
+        settle(send_sem.at[1], msg2, n_ctx - 1)
+        settle(send_sem.at[2], gather1, len(second_set) * held)
+
+    settle(send_sem.at[3], gather2, len(third_set))
 
 
 def write_out(wide, small, out_conv, out_left, out_right, out_values, out_res, out_rate, sem):
-    tiles = wide.shape[1]
     copies = [
-        pltpu.make_async_copy(wide.at[a, j], ref.at[:, pl.ds(j * TILE, TILE)], sem)
-        for a, ref in enumerate((out_conv, out_left, out_right, out_values))
-        for j in range(tiles)
-    ] + [pltpu.make_async_copy(small.at[k], ref, sem) for k, ref in enumerate((out_res, out_rate))]
+        pltpu.make_async_copy(src, ref, sem)
+        for src, ref in (
+            (small.at[0], out_res),
+            (small.at[1], out_rate),
+            (wide.at[0], out_conv),
+            (wide.at[1], out_left),
+            (wide.at[2], out_right),
+            (wide.at[3], out_values),
+        )
+    ]
     for copy in copies:
         copy.start()
     pltpu.make_async_copy(wide, wide, sem).wait()
@@ -400,6 +476,7 @@
         positions, channels = left_gate.shape[1:]
         tiles = channels // TILE
         groups = channels // GSIZE
+        held = groups // (n_ctx // N_Z * (N_Z - 2))
         flat = [x.reshape(positions, channels) for x in (left_gate, right_gate, values, grad_out)]
         wide = jax.ShapeDtypeStruct((positions, channels), BF)
         small = jax.ShapeDtypeStruct(residues.shape[::-1], F32)
@@ -408,24 +485,25 @@
         outs = pl.pallas_call(
             functools.partial(kernel, n_ctx, N_Z, n_tensor, N_CORE, n_dp),
             out_shape=(
-                jax.ShapeDtypeStruct((4, tiles, positions, TILE), BF),
+                jax.ShapeDtypeStruct((4, positions, channels), BF),
                 jax.ShapeDtypeStruct((2,) + residues.shape[::-1], F32),
             ),
             in_specs=[in_hbm] * 6,
             out_specs=(in_vmem, in_vmem),
             scratch_shapes=[
-                pltpu.VMEM((4, tiles, positions, TILE), BF),
+                pltpu.VMEM((4, positions, channels), BF),
                 pltpu.VMEM((2,) + residues.shape, F32),
                 pltpu.VMEM((4, tiles, TILE, TILE), BF),
                 pltpu.VMEM((tiles, 6, positions, TILE), BF),
                 pltpu.VMEM((tiles, PER_TILE, positions), F32),
                 pltpu.VMEM((2, tiles, TILE, positions), F32),
-                pltpu.VMEM((n_ctx, 9, TILE), F32),
-                pltpu.VMEM((n_ctx, 9, TILE), F32),
-                pltpu.VMEM((n_ctx, 8, TILE), F32),
-                pltpu.VMEM((n_ctx, 8, TILE), F32),
-                pltpu.VMEM((1, TILE), F32),
-                pltpu.VMEM((n_dp * n_tensor // N_CORE * N_Z, 1, TILE), F32),
+                pltpu.VMEM((groups, 9, TILE), F32),
+                pltpu.VMEM((n_ctx, held, 9, TILE), F32),
+                pltpu.VMEM((held, n_ctx, 8, TILE), F32),
+                pltpu.VMEM((n_ctx, held, 4, TILE), F32),
+                pltpu.VMEM((groups // held, held, 4, TILE), F32),
+                pltpu.VMEM((held, 1, TILE), F32),
+                pltpu.VMEM((n_dp * n_tensor // N_CORE * N_Z * held, 1, TILE), F32),
                 pltpu.VMEM((N_Z, TILE), F32),
                 pltpu.VMEM((n_ctx // N_Z * N_CORE, N_Z, TILE), F32),
                 pltpu.SemaphoreType.DMA,

time: 36.1 us -> 34.9 us (0.967)
  Pallas kernels: 35.2 us -> 34.1 us
    pallas_call x1, Pallas kernels: 34.4 us -> 33.3 us  [on_device(): pl.pallas_call(functools.partial(kernel, n_ctx, N_Z, n_tensor, N_CORE, n_...]
where the time goes in v2:
time: 34.9 us; the launch traced here: 34.8 us
  Pallas kernels  34.1 us (98%)
  between operations  0.64 us (2%)
    pallas_call x1, Pallas kernels, on_device(): pl.pallas_call(functools.partial(kernel, n_ctx, N_Z, n_tensor, N_CORE, n_...  33.3 us
    pallas_call x1, Pallas kernels, on_device(): pl.pallas_call(write_out, out_shape=(wide, wide, wide, wide, small, small...  0.8 us

profile of v2, /device:TPU:1, one launch (start us, length us, event | category | flops | bytes accessed | tf_op | source)
XLA Modules:
  0.0 34.8 jit_solution(6442352159833418050)
XLA Ops:
  0.6 33.3 %shard_map.109 = (bf16[4,128,512]{2,1,0:T(8,128)(2,1)S(1)}, f32[2,16,256]{2,1,0:T(8,128)S(1)}) custom-call(bf16[128,512]{1,0:T(8,128)(2,1)} %bitcast.12, bf16[128,512]{1,0:T(8,128)(2,1)} %bitcast.13, bf16[128,512]{1,0:T(8,128)(2,1)} %bitcast.14, bf16[128,512]{1,0:T(8,128)(2,1)} %bitcast.15, f32[16,256]{1,0:T(8,128)} %bitcast.16, f32[16,256]{1,0:T(8,128)} %bitcast.17), custom_call_target="tpu_custom_call" | custom-call | tf_op jit(solution)/shard_map/pallas_call | solution.py:485
  34.0 0.8 %shard_map.110 = (bf16[128,512]{1,0:T(8,128)(2,1)}, bf16[128,512]{1,0:T(8,128)(2,1)}, bf16[128,512]{1,0:T(8,128)(2,1)}, bf16[128,512]{1,0:T(8,128)(2,1)}, f32[16,256]{1,0:T(8,128)}, /*index=5*/f32[16,256]{1,0:T(8,128)}) custom-call(bf16[4,128,512]{2,1,0:T(8,128)(2,1)S(1)} %get-tuple-element.14.wide, f32[2,16,256]{2,1,0:T(8,128)S(1)} %get-tuple-element.15.small), custom_call_target="tpu_custom_call" | custom-call | tf_op jit(solution)/shard_map/pallas_call | solution.py:518

commit v3 on v2

--- a/solution.py
+++ b/solution.py
@@ -76,6 +76,7 @@
     msg1,
     recv1,
     hold,
+    fronts,
     msg2,
     recv2,
     grad1,
@@ -319,31 +320,29 @@
             decay_d = decays(rate_d, positions, positions - 1)
             local.append((rate_d, res_d, decay_d, (block - at) & 3))
         settle(recv_sem.at[0], recv1, n_ctx - 1)
+        zero = jnp.zeros((8, TILE), F32)
+        decs = [jnp.exp(-local[k][0] * positions) for k in range(held)]
+        back = [zero] * held
+        for i in reversed(range(n_ctx)):
+            for k in range(held):
+                hold[k, i] = back[k]
+                back[k] = back[k] * decs[k] + recv1[i, k, 0:8, :]
+        front, sums_r, sums_s, sums_m = [zero] * held, [zero] * held, [zero] * held, [zero] * held
+        for i in range(n_ctx):
+            for k in range(held):
+                kind = local[k][3]
+                mine = recv1[i, k, 0:8, :]
+                behind = hold[k, i]
+                mixed = shift(jnp.where(kind == 2, mine, behind), 96)
+                sums_r[k] = sums_r[k] + front[k] * shift(mine, 80)
+                sums_m[k] = sums_m[k] + front[k] * shift(behind, 80)
+                sums_s[k] = sums_s[k] + jnp.where(kind == 0, front[k], mine) * mixed
+                fronts[k, i] = front[k]
+                front[k] = front[k] * decs[k] + mine
         for k in range(held):
             rate_d, res_d, decay_d, kind = local[k]
-            dec = jnp.exp(-rate_d * positions)
-            is0, is1, is2, is3 = [kind == v for v in range(4)]
-            outer = is0 | is3
-            back = jnp.zeros((8, TILE), F32)
-            for i in reversed(range(n_ctx)):
-                hold[k, i] = back
-                back = back * dec + recv1[i, k, 0:8, :]
-            front = jnp.zeros((8, TILE), F32)
-            sum_r = jnp.zeros((8, TILE), F32)
-            sum_s = jnp.zeros((8, TILE), F32)
-            sum_m = jnp.zeros((8, TILE), F32)
-            for i in range(n_ctx):
-                mine = recv1[i, k, 0:8, :]
-                behind = hold[k, i]
-                behind0 = shift(behind, 80)
-                mixed = shift(jnp.where(is2, mine, behind), 96)
-                sum_r = sum_r + front * shift(mine, 80)
-                sum_m = sum_m + front * behind0
-                sum_s = sum_s + jnp.where(is0, front, mine) * mixed
-                both = jnp.where(is0, behind0, shift(front, 48)) * res_d
-                low = shift(pltpu.roll(both, 4, 0), 32)
-                msg2[i, k] = jnp.where(outer, both, low)[0:4]
-                front = front * dec + mine
+            dec, sum_r, sum_s, sum_m = decs[k], sums_r[k], sums_s[k], sums_m[k]
+            is0, is1 = kind == 0, kind == 1
 
             def fold(x):
                 x = jnp.sum(x, axis=0, keepdims=True)
@@ -371,6 +370,13 @@
         for where in second_set:
             send(grad1, gather1.at[pl.ds(slot, held)], where, 2)
         gather1[pl.ds(slot, held)] = grad1[...]
+        for k in range(held):
+            _, res_d, _, kind = local[k]
+            outer = (kind == 0) | (kind == 3)
+            for i in range(n_ctx):
+                both = jnp.where(kind == 0, shift(hold[k, i], 80), shift(fronts[k, i], 48)) * res_d
+                low = shift(pltpu.roll(both, 4, 0), 32)
+                msg2[i, k] = jnp.where(outer, both, low)[0:4]
         for peer in line:
             send(msg2.at[peer], recv2.at[my_owner], {"ctx": peer}, 1)
         recv2[my_owner] = msg2[me]
@@ -435,12 +441,12 @@
     every = jnp.concatenate([gather2[i] for i in range(n_y * n_core)], axis=0)
     total = jnp.sum(jnp.sum(every * every, axis=0, keepdims=True), axis=1, keepdims=True)
     factor = CLIP / jnp.maximum(jnp.sqrt(total), CLIP)
-    turned = (every * factor).T
+    turned = every.T
     span = n_y * n_core * n_z
     for x in range(n_x):
         for k in range(2):
             at = x * 32 + k * ORD
-            gout[k, :, x * span : (x + 1) * span] = turned[at : at + ORD]
+            gout[k, :, x * span : (x + 1) * span] = turned[at : at + ORD] * factor
     by_role(send_sem.at[0], recv1, n_owner - 1, n_owner)
 
     @pl.when(own)
@@ -500,6 +506,7 @@
                 pltpu.VMEM((groups, 9, TILE), F32),
                 pltpu.VMEM((n_ctx, held, 9, TILE), F32),
                 pltpu.VMEM((held, n_ctx, 8, TILE), F32),
+                pltpu.VMEM((held, n_ctx, 8, TILE), F32),
                 pltpu.VMEM((n_ctx, held, 4, TILE), F32),
                 pltpu.VMEM((groups // held, held, 4, TILE), F32),
                 pltpu.VMEM((held, 1, TILE), F32),

time: 34.9 us -> 34.6 us (level)
  no operation moved by 1% of the time
where the time goes in v3:
time: 34.6 us; the launch traced here: 34.5 us
  Pallas kernels  33.8 us (98%)
  between operations  0.64 us (2%)
    pallas_call x1, Pallas kernels, on_device(): pl.pallas_call(functools.partial(kernel, n_ctx, N_Z, n_tensor, N_CORE, n_...  33 us
    pallas_call x1, Pallas kernels, on_device(): pl.pallas_call(write_out, out_shape=(wide, wide, wide, wide, small, small...  0.8 us

profile of v3, /device:TPU:1, one launch (start us, length us, event | category | flops | bytes accessed | tf_op | source)
XLA Modules:
  0.0 34.5 jit_solution(5881425203039370281)
XLA Ops:
  0.6 33.0 %shard_map.109 = (bf16[4,128,512]{2,1,0:T(8,128)(2,1)S(1)}, f32[2,16,256]{2,1,0:T(8,128)S(1)}) custom-call(bf16[128,512]{1,0:T(8,128)(2,1)} %bitcast.12, bf16[128,512]{1,0:T(8,128)(2,1)} %bitcast.13, bf16[128,512]{1,0:T(8,128)(2,1)} %bitcast.14, bf16[128,512]{1,0:T(8,128)(2,1)} %bitcast.15, f32[16,256]{1,0:T(8,128)} %bitcast.16, f32[16,256]{1,0:T(8,128)} %bitcast.17), custom_call_target="tpu_custom_call" | custom-call | tf_op jit(solution)/shard_map/pallas_call | solution.py:491
  33.6 0.8 %shard_map.110 = (bf16[128,512]{1,0:T(8,128)(2,1)}, bf16[128,512]{1,0:T(8,128)(2,1)}, bf16[128,512]{1,0:T(8,128)(2,1)}, bf16[128,512]{1,0:T(8,128)(2,1)}, f32[16,256]{1,0:T(8,128)}, /*index=5*/f32[16,256]{1,0:T(8,128)}) custom-call(bf16[4,128,512]{2,1,0:T(8,128)(2,1)S(1)} %get-tuple-element.14.wide, f32[2,16,256]{2,1,0:T(8,128)S(1)} %get-tuple-element.15.small), custom_call_target="tpu_custom_call" | custom-call | tf_op jit(solution)/shard_map/pallas_call | solution.py:525

commit v4 on v3

--- a/solution.py
+++ b/solution.py
@@ -437,6 +437,13 @@
     for j in range(tiles):
         finish(j, 0)
 
+    by_role(send_sem.at[0], recv1, n_owner - 1, n_owner)
+
+    @pl.when(own)
+    def _():
+        settle(send_sem.at[1], msg2, n_ctx - 1)
+        settle(send_sem.at[2], gather1, len(second_set) * held)
+
     settle(recv_sem.at[3], gather2, len(third_set))
     every = jnp.concatenate([gather2[i] for i in range(n_y * n_core)], axis=0)
     total = jnp.sum(jnp.sum(every * every, axis=0, keepdims=True), axis=1, keepdims=True)
@@ -447,13 +454,6 @@
         for k in range(2):
             at = x * 32 + k * ORD
             gout[k, :, x * span : (x + 1) * span] = turned[at : at + ORD] * factor
-    by_role(send_sem.at[0], recv1, n_owner - 1, n_owner)
-
-    @pl.when(own)
-    def _():
-        settle(send_sem.at[1], msg2, n_ctx - 1)
-        settle(send_sem.at[2], gather1, len(second_set) * held)
-
     settle(send_sem.at[3], gather2, len(third_set))
 
 

time: 34.6 us -> 34.6 us (level)
  no operation moved by 1% of the time
where the time goes in v4:
time: 34.6 us; the launch traced here: 34.5 us
  Pallas kernels  33.8 us (98%)
  between operations  0.64 us (2%)
    pallas_call x1, Pallas kernels, on_device(): pl.pallas_call(functools.partial(kernel, n_ctx, N_Z, n_tensor, N_CORE, n_...  33 us
    pallas_call x1, Pallas kernels, on_device(): pl.pallas_call(write_out, out_shape=(wide, wide, wide, wide, small, small...  0.8 us

profile of v4, /device:TPU:1, one launch (start us, length us, event | category | flops | bytes accessed | tf_op | source)
XLA Modules:
  0.0 34.5 jit_solution(1125323078194937151)
XLA Ops:
  0.6 33.0 %shard_map.109 = (bf16[4,128,512]{2,1,0:T(8,128)(2,1)S(1)}, f32[2,16,256]{2,1,0:T(8,128)S(1)}) custom-call(bf16[128,512]{1,0:T(8,128)(2,1)} %bitcast.12, bf16[128,512]{1,0:T(8,128)(2,1)} %bitcast.13, bf16[128,512]{1,0:T(8,128)(2,1)} %bitcast.14, bf16[128,512]{1,0:T(8,128)(2,1)} %bitcast.15, f32[16,256]{1,0:T(8,128)} %bitcast.16, f32[16,256]{1,0:T(8,128)} %bitcast.17), custom_call_target="tpu_custom_call" | custom-call | tf_op jit(solution)/shard_map/pallas_call | solution.py:491
  33.6 0.8 %shard_map.110 = (bf16[128,512]{1,0:T(8,128)(2,1)}, bf16[128,512]{1,0:T(8,128)(2,1)}, bf16[128,512]{1,0:T(8,128)(2,1)}, bf16[128,512]{1,0:T(8,128)(2,1)}, f32[16,256]{1,0:T(8,128)}, /*index=5*/f32[16,256]{1,0:T(8,128)}) custom-call(bf16[4,128,512]{2,1,0:T(8,128)(2,1)S(1)} %get-tuple-element.14.wide, f32[2,16,256]{2,1,0:T(8,128)S(1)} %get-tuple-element.15.small), custom_call_target="tpu_custom_call" | custom-call | tf_op jit(solution)/shard_map/pallas_call | solution.py:525
